TPU v7x, 128 devices: a whole 4x4x4 slice. The times are simulated.
128 devices in a mesh: sections: 4 (over x), cache: 16 (over z, y), heads: 2 (over core).
Axes of the slice: x: 4, y: 4, z: 4, core: 2. Of those that a mesh axis runs over, the one named last changes fastest.
Arguments:
- hidden: bfloat16 [4, 4096, 2048], P('sections', 'cache'), may hold values from -6 to 6
- norm_gain: float32 [4, 2048], P('sections'), may hold values from 0.1 to 1.9
- w_query: bfloat16 [4, 2048, 4096], P('sections', None, 'heads'), may hold values from -0.125 to 0.125
- query_gain: float32 [4, 128], P('sections'), may hold values from 0.1 to 1.9
- w_output: bfloat16 [4, 4096, 2048], P('sections', 'heads'), may hold values from -0.09375 to 0.09375
- key_cache: bfloat16 [4, 512, 64, 512], P('sections', 'cache', None, 'heads'), may hold values from -6 to 6
- value_cache: bfloat16 [4, 512, 64, 512], P('sections', 'cache', None, 'heads'), may hold values from -6 to 6
- key_scale: float32 [4, 512, 4], P('sections', 'cache', 'heads'), may hold values from 0.5 to 120
- value_scale: float32 [4, 512, 4], P('sections', 'cache', 'heads'), may hold values from 0.5 to 2
- page_table: int32 [512], replicated, may hold values from 0 to 511, as said below
- page_tokens: int32 [512], replicated, may hold values from 1 to 64
- page_list: int32 [4, 32, 64], P('sections'), may hold values from 0 to 511, as said below
- list_len: int32 [4, 32], P('sections'), may hold values from 32 to 64, as said below
Outputs:
- mixed: bfloat16 [4, 4096, 2048], P('sections', 'cache', 'heads')
Inputs may be any that keep to these rules, and one draw needn't show every extreme that they name: `page_table`: A permutation of the 512 slots; slot // 32 is the cache index that holds the page. `page_list`: the 64 entries of a block are distinct logical pages; among them at most 8 have their slot on any one cache index, and in every block some cache index holds exactly 8 of them. Entries of a list from list_len on are unused; some block uses all 64 entries.
All inputs are finite; a program needn't handle non-finite values.
Results may differ from a plain program's by a relative error of at most 0.008.
The roundings to bfloat16 on the way count: a program that leaves them out, or rounds other values in their place, can miss the bound.
Values may be sent and summed in bfloat16 or wider, within the bound.
No kernel may reach another device: no remote copies, remote signals or barrier semaphores. Data moves between devices by JAX's collectives and lax.ppermute only.
A program may use at most 128 MiB of HBM per device.

v0:
```python
import math

import jax
import jax.numpy as jnp
from jax import lax
from jax.sharding import PartitionSpec as P

QBLOCK = 128
QB_DEV = 2
MOST = 8


tiny_eps = 1e-06
masked_score = -1e30


def side_by_side(arrays, axis, dim, along):
    widths = [a.shape[along] for a in arrays]
    both = jnp.concatenate(arrays, axis=along)
    whole = lax.all_gather(both, axis, axis=dim, tiled=True)
    return tuple(jnp.split(whole, [sum(widths[:k]) for k in range(1, len(widths))], axis=along))


def cut_along(x, dim, devices):
    lengths = x.shape
    parts = x.reshape(*lengths[:dim], devices, lengths[dim] // devices, *lengths[dim + 1 :])
    return jnp.moveaxis(parts, dim, 0)


def sum_at_owner(x, axis, dim):
    parts = cut_along(x, dim, lax.axis_size(axis))
    arrived = lax.all_to_all(parts, axis, split_axis=0, concat_axis=0, tiled=True)
    return arrived.astype(jnp.float32).sum(axis=0)


def shifted(block, axis, distance):
    devices = range(lax.axis_size(axis))
    route = [((i - distance) % len(devices), i) for i in devices]
    return lax.ppermute(block, axis, route)


def lookup(entries, table):
    places = jnp.arange(table.shape[0], dtype=jnp.int32)
    matches = (entries[..., None] == places).astype(jnp.int32)
    return jnp.sum(matches * table, axis=-1)


def plan_pages(slots, counts, length, target, pages_dev):
    listed = slots.shape[-1]
    order = jnp.arange(listed, dtype=jnp.int32)
    chosen = (slots // pages_dev == target) & (order < length)
    flags = chosen.astype(jnp.int32)
    ranks = jnp.cumsum(flags) - flags
    wanted = jnp.arange(MOST, dtype=jnp.int32)
    picks = ((ranks[None, :] == wanted[:, None]) & chosen[None, :]).astype(jnp.int32)
    local = jnp.sum(picks * (slots % pages_dev)[None, :], axis=1)
    filled = jnp.sum(picks * counts[None, :], axis=1)
    return (local, filled)


def plan_blocks(slots, counts, lengths, target, pages_dev):
    return jax.vmap(
        lambda one_slots, one_counts, one_length: plan_pages(
            one_slots, one_counts, one_length, target, pages_dev
        )
    )(slots, counts, lengths)


def prepare(key_pages, value_pages, key_scales, value_scales, filled, kv_local, head_size):
    blocks_here, page_slots, page_len, merged = key_pages.shape
    key_span = page_slots * page_len
    key_rows = key_pages.reshape(blocks_here, key_span, kv_local, head_size)
    value_rows = value_pages.reshape(blocks_here, key_span, kv_local, head_size)
    key_factor = jnp.repeat(jnp.swapaxes(key_scales, 1, 2), page_len, axis=2)
    value_factor = jnp.repeat(jnp.swapaxes(value_scales, 1, 2), page_len, axis=2)
    within = jnp.arange(page_len, dtype=jnp.int32)
    live_mask = (within[None, None, :] < filled[:, :, None]).reshape(blocks_here, key_span)
    return (key_rows, value_rows, key_factor, value_factor, live_mask)


def attend(softmax_state, queries, prepared):
    key_rows, value_rows, key_factor, value_factor, live_mask = prepared
    top_score, totals, accumulated = softmax_state
    scores = (
        jnp.einsum("bgqd,btgd->bgqt", queries, key_rows, preferred_element_type=jnp.float32)
        * key_factor[:, :, None, :]
    )
    keeper = live_mask[:, None, None, :]
    scores = jnp.where(keeper, scores, masked_score)
    new_top = jnp.maximum(top_score, jnp.max(scores, axis=-1))
    weights = jnp.where(keeper, jnp.exp(scores - new_top[..., None]), 0.0)
    rescale = jnp.exp(top_score - new_top)
    totals = totals * rescale + jnp.sum(weights, axis=-1)
    scaled = (weights * value_factor[:, :, None, :]).astype(jnp.bfloat16)
    accumulated = accumulated * rescale[..., None] + jnp.einsum(
        "bgqt,btgd->bgqd", scaled, value_rows, preferred_element_type=jnp.float32
    )
    return (new_top, totals, accumulated)


def body(
    hidden,
    norm_gain,
    w_query,
    query_gain,
    w_output,
    key_cache,
    value_cache,
    key_scale,
    value_scale,
    page_table,
    page_tokens,
    page_list,
    list_len,
):
    row_count = hidden.shape[1]
    model_width = hidden.shape[2]
    head_size = query_gain.shape[1]
    kv_local = key_scale.shape[2]
    heads_local = w_query.shape[2] // head_size
    group_size = heads_local // kv_local
    pages_dev = key_cache.shape[1]
    shard_count = lax.axis_size("cache")
    own_shard = lax.axis_index("cache")
    inputs = hidden[0].astype(jnp.float32)
    inverse = lax.rsqrt(jnp.mean(inputs * inputs, axis=-1, keepdims=True) + tiny_eps)
    normed = (
        (inputs * inverse * norm_gain[0]).astype(jnp.bfloat16).reshape(QB_DEV, QBLOCK, model_width)
    )
    projected = jnp.einsum(
        "bre,ehd->bhrd",
        normed,
        w_query[0].reshape(model_width, heads_local, head_size),
        preferred_element_type=jnp.float32,
    )
    head_inverse = lax.rsqrt(jnp.mean(projected * projected, axis=-1, keepdims=True) + tiny_eps)
    queries = (projected * head_inverse * query_gain[0] / math.sqrt(head_size)).astype(jnp.bfloat16)
    queries = queries.reshape(QB_DEV, kv_local, group_size * QBLOCK, head_size)
    all_slots = lookup(page_list[0], page_table)
    all_counts = lookup(page_list[0], page_tokens)
    all_lengths = list_len[0]
    state_shape = (QB_DEV, kv_local, group_size * QBLOCK)
    initial_state = (
        jnp.full(state_shape, masked_score, jnp.float32),
        jnp.zeros(state_shape, jnp.float32),
        jnp.zeros(state_shape + (head_size,), jnp.float32),
    )
    local_all, filled_all = plan_blocks(all_slots, all_counts, all_lengths, own_shard, pages_dev)
    page_shape = (shard_count, QB_DEV) + local_all.shape[1:] + key_cache.shape[2:]
    outgoing_keys = key_cache[0][local_all].reshape(page_shape)
    outgoing_values = value_cache[0][local_all].reshape(page_shape)
    incoming_keys, incoming_values = (
        lax.all_to_all(outgoing_keys, "cache", split_axis=0, concat_axis=0, tiled=True),
        lax.all_to_all(outgoing_values, "cache", split_axis=0, concat_axis=0, tiled=True),
    )
    key_table, value_table = side_by_side((key_scale, value_scale), "cache", 1, 0)
    first_block = own_shard * QB_DEV
    own_slots = lax.dynamic_slice_in_dim(all_slots, first_block, QB_DEV, 0)
    own_counts = lax.dynamic_slice_in_dim(all_counts, first_block, QB_DEV, 0)
    own_lengths = lax.dynamic_slice_in_dim(all_lengths, first_block, QB_DEV, 0)
    sources = jnp.arange(shard_count, dtype=jnp.int32)
    local_src, filled_src = jax.vmap(
        lambda source: plan_blocks(own_slots, own_counts, own_lengths, source, pages_dev)
    )(sources)
    global_slot = sources[:, None, None] * pages_dev + local_src
    page_ids = jnp.arange(key_table.shape[1], dtype=jnp.int32)
    one_hot = (global_slot[..., None] == page_ids).astype(jnp.float32)
    key_scales_src = jnp.einsum(
        "nbmp,pk->nbmk", one_hot, key_table[0], precision=lax.Precision.HIGHEST
    )
    value_scales_src = jnp.einsum(
        "nbmp,pk->nbmk", one_hot, value_table[0], precision=lax.Precision.HIGHEST
    )

    def fetch_step(source, softmax_state):

        def select_row(stacked):
            return lax.dynamic_index_in_dim(stacked, source, 0, keepdims=False)

        prepared = prepare(
            select_row(incoming_keys),
            select_row(incoming_values),
            select_row(key_scales_src),
            select_row(value_scales_src),
            select_row(filled_src),
            kv_local,
            head_size,
        )
        return attend(softmax_state, queries, prepared)

    softmax_state = lax.fori_loop(0, shard_count, fetch_step, initial_state)
    top_score, totals, accumulated = softmax_state
    attended = (
        (accumulated / totals[..., None])
        .astype(jnp.bfloat16)
        .reshape(QB_DEV, heads_local, QBLOCK, head_size)
    )
    partial_value = jnp.einsum(
        "bhrd,hde->bre",
        attended,
        w_output[0].reshape(heads_local, head_size, model_width),
        preferred_element_type=jnp.float32,
    ).reshape(row_count, model_width)
    summed = sum_at_owner(partial_value.astype(jnp.bfloat16), "heads", 1)
    half_width = summed.shape[1]
    residual = lax.dynamic_slice_in_dim(inputs, lax.axis_index("heads") * half_width, half_width, 1)
    result = (summed + residual).astype(jnp.bfloat16)
    return shifted(result[None], "sections", 1)


def solution(mesh):
    return jax.shard_map(
        body,
        mesh=mesh,
        in_specs=(
            P("sections", "cache", None),
            P("sections", None),
            P("sections", None, "heads"),
            P("sections", None),
            P("sections", "heads", None),
            P("sections", "cache", None, "heads"),
            P("sections", "cache", None, "heads"),
            P("sections", "cache", "heads"),
            P("sections", "cache", "heads"),
            P(),
            P(),
            P("sections", None, None),
            P("sections", None),
        ),
        out_specs=P("sections", "cache", "heads"),
        check_vma=False,
    )
```

profile of v0, /device:TPU:1, one launch (start us, length us, event | category | flops | bytes accessed | tf_op | source)
XLA Modules:
  0.0 617.8 jit_solution(7160201255941767624)
XLA Ops:
  0.0 2.9 select_reduce_fusion.1
  4.6 8.4 %gather_fusion = bf16[256,64,256]{2,1,0:T(8,128)(2,1)} fusion(bf16[32,64,256]{2,1,0:T(8,128)(2,1)S(1)} %bitcast.125, s32[1024]{0:T(1024)S(1)} %pad_clamp_fusion), kind=kCustom, calls=%fused_computation | custom fusion | bytes 16778240 | tf_op jit(solution)/shard_map/gather | solution.py:150
  13.0 8.8 %all-to-all-start = ((bf16[16,2,8,64,256]{4,3,2,1,0:T(8,128)(2,1)}), bf16[16,2,8,64,256]{4,3,2,1,0:T(8,128)(2,1)}, u32[]{:S(2)}, u32[]{:S(2)}) async-start(bf16[16,2,8,64,256]{4,3,2,1,0:T(8,128)(2,1)} %bitcast.129), calls=%async_computation | async-start | bytes 16777216 | tf_op jit(solution)/shard_map/all_to_all | solution.py:153
  21.8 8.4 %gather_fusion.1 = bf16[256,64,256]{2,1,0:T(8,128)(2,1)} fusion(bf16[32,64,256]{2,1,0:T(8,128)(2,1)S(1)} %bitcast.126, s32[1024]{0:T(1024)S(1)} %pad_clamp_fusion), kind=kCustom, calls=%fused_computation.1 | custom fusion | bytes 16778240 | tf_op jit(solution)/shard_map/gather | solution.py:151
  30.1 114.7 %all-to-all-done = bf16[16,2,8,64,256]{4,3,2,1,0:T(8,128)(2,1)} async-done(((bf16[16,2,8,64,256]{4,3,2,1,0:T(8,128)(2,1)}), bf16[16,2,8,64,256]{4,3,2,1,0:T(8,128)(2,1)}, u32[]{:S(2)}, u32[]{:S(2)}) %all-to-all-start) | async-done | bytes 8388640 | tf_op jit(solution)/shard_map/all_to_all | solution.py:153
  144.9 5.6 all-to-all-start.1
  151.4 9.8 %copy.67 = bf16[256,8,16,128]{3,2,1,0:T(8,128)(2,1)} copy(bf16[256,8,16,128]{3,1,2,0:T(8,128)(2,1)} %bitcast.130) | data formatting | bytes 16777216
  162.8 120.5 %all_gather.3 = f32[2,512,2]{2,0,1:T(2,128)S(1)} all-gather(f32[2,32,2]{2,0,1:T(2,128)S(1)} %copy.55), channel_id=1, replica_groups=mesh['sections'=4,'cache'=16,'heads'=2] {'cache'}, dimensions={1}, use_global_device_ids=true | all-gather | bytes 8704 | tf_op jit(solution)/shard_map/all_gather | solution.py:20
  285.1 5.9 fusion.19
  291.6 1.9 fusion.25
  293.5 1.9 fusion.26
  296.3 288.0 %while.18 = (s32[]{:T(128)}, f32[2,2,1024]{2,1,0:T(2,128)S(1)}, f32[2,2,1024]{2,1,0:T(2,128)S(1)}, f32[2,2,1024,128]{3,2,1,0:T(8,128)}, s32[16,2,8]{2,1,0:T(2,12...) while((s32[]{:T(128)}, f32[2,2,1024]{2,1,0:T(2,128)S(1)}, ...), condition=%wide.region_12.13_spmd.clone, body=%wide.region_9.12_spmd.clone.sunk | while | flops 1104696320 | bytes 36025420 | solution.py:191
  298.2 4.0 bitcast_reduce_fusion.2
  302.2 4.6 fusion.58
  307.1 7.0 %fusion.60 = f32[2,2,1024,128]{3,2,1,0:T(8,128)} fusion(f32[2,2,1024,128]{3,2,1,0:T(8,128)} %get-tuple-element.347, f32[2,2,512,1024]{3,2,1,0:T(8,128)} %get-tuple-element.327, f32[2,2,512]{2,1,0:T(2,128)S(1)} %mul.310, f32[2,2,1024]{2,1,0:T(2,128)S(1)} %fusion.57, f32[2,2,512]{2,1,0:T(2,128)S(1)} %mul.309, ...), kind=kOutput, calls=%fused_computation.13.clone.1 | convolution fusion | flops 551026688 | bytes 13157377 | tf_op jit(solution)/shard_map/while/body/eval_jaxpr/bgqt,btgd->bgqd/dot_general | solution.py:95
  315.9 4.0 bitcast_reduce_fusion.2
  319.9 4.6 fusion.58
  324.8 7.3 %fusion.60 = f32[2,2,1024,128]{3,2,1,0:T(8,128)} fusion(f32[2,2,1024,128]{3,2,1,0:T(8,128)} %get-tuple-element.347, f32[2,2,512,1024]{3,2,1,0:T(8,128)} %get-tuple-element.327, f32[2,2,512]{2,1,0:T(2,128)S(1)} %mul.310, f32[2,2,1024]{2,1,0:T(2,128)S(1)} %fusion.57, f32[2,2,512]{2,1,0:T(2,128)S(1)} %mul.309, ...), kind=kOutput, calls=%fused_computation.13.clone.1 | convolution fusion | flops 551026688 | bytes 13157377 | tf_op jit(solution)/shard_map/while/body/eval_jaxpr/bgqt,btgd->bgqd/dot_general | solution.py:95
  333.9 4.0 bitcast_reduce_fusion.2
  337.9 4.6 fusion.58
  342.8 7.3 %fusion.60 = f32[2,2,1024,128]{3,2,1,0:T(8,128)} fusion(f32[2,2,1024,128]{3,2,1,0:T(8,128)} %get-tuple-element.347, f32[2,2,512,1024]{3,2,1,0:T(8,128)} %get-tuple-element.327, f32[2,2,512]{2,1,0:T(2,128)S(1)} %mul.310, f32[2,2,1024]{2,1,0:T(2,128)S(1)} %fusion.57, f32[2,2,512]{2,1,0:T(2,128)S(1)} %mul.309, ...), kind=kOutput, calls=%fused_computation.13.clone.1 | convolution fusion | flops 551026688 | bytes 13157377 | tf_op jit(solution)/shard_map/while/body/eval_jaxpr/bgqt,btgd->bgqd/dot_general | solution.py:95
  351.9 4.0 bitcast_reduce_fusion.2
  355.9 4.6 fusion.58
  360.8 7.3 %fusion.60 = f32[2,2,1024,128]{3,2,1,0:T(8,128)} fusion(f32[2,2,1024,128]{3,2,1,0:T(8,128)} %get-tuple-element.347, f32[2,2,512,1024]{3,2,1,0:T(8,128)} %get-tuple-element.327, f32[2,2,512]{2,1,0:T(2,128)S(1)} %mul.310, f32[2,2,1024]{2,1,0:T(2,128)S(1)} %fusion.57, f32[2,2,512]{2,1,0:T(2,128)S(1)} %mul.309, ...), kind=kOutput, calls=%fused_computation.13.clone.1 | convolution fusion | flops 551026688 | bytes 13157377 | tf_op jit(solution)/shard_map/while/body/eval_jaxpr/bgqt,btgd->bgqd/dot_general | solution.py:95
  369.9 4.0 bitcast_reduce_fusion.2
  373.9 4.6 fusion.58
  378.8 7.3 %fusion.60 = f32[2,2,1024,128]{3,2,1,0:T(8,128)} fusion(f32[2,2,1024,128]{3,2,1,0:T(8,128)} %get-tuple-element.347, f32[2,2,512,1024]{3,2,1,0:T(8,128)} %get-tuple-element.327, f32[2,2,512]{2,1,0:T(2,128)S(1)} %mul.310, f32[2,2,1024]{2,1,0:T(2,128)S(1)} %fusion.57, f32[2,2,512]{2,1,0:T(2,128)S(1)} %mul.309, ...), kind=kOutput, calls=%fused_computation.13.clone.1 | convolution fusion | flops 551026688 | bytes 13157377 | tf_op jit(solution)/shard_map/while/body/eval_jaxpr/bgqt,btgd->bgqd/dot_general | solution.py:95
  387.9 4.0 bitcast_reduce_fusion.2
  392.0 4.6 fusion.58
  396.8 7.3 %fusion.60 = f32[2,2,1024,128]{3,2,1,0:T(8,128)} fusion(f32[2,2,1024,128]{3,2,1,0:T(8,128)} %get-tuple-element.347, f32[2,2,512,1024]{3,2,1,0:T(8,128)} %get-tuple-element.327, f32[2,2,512]{2,1,0:T(2,128)S(1)} %mul.310, f32[2,2,1024]{2,1,0:T(2,128)S(1)} %fusion.57, f32[2,2,512]{2,1,0:T(2,128)S(1)} %mul.309, ...), kind=kOutput, calls=%fused_computation.13.clone.1 | convolution fusion | flops 551026688 | bytes 13157377 | tf_op jit(solution)/shard_map/while/body/eval_jaxpr/bgqt,btgd->bgqd/dot_general | solution.py:95
  406.0 4.0 bitcast_reduce_fusion.2
  410.0 4.6 fusion.58
  414.9 7.3 %fusion.60 = f32[2,2,1024,128]{3,2,1,0:T(8,128)} fusion(f32[2,2,1024,128]{3,2,1,0:T(8,128)} %get-tuple-element.347, f32[2,2,512,1024]{3,2,1,0:T(8,128)} %get-tuple-element.327, f32[2,2,512]{2,1,0:T(2,128)S(1)} %mul.310, f32[2,2,1024]{2,1,0:T(2,128)S(1)} %fusion.57, f32[2,2,512]{2,1,0:T(2,128)S(1)} %mul.309, ...), kind=kOutput, calls=%fused_computation.13.clone.1 | convolution fusion | flops 551026688 | bytes 13157377 | tf_op jit(solution)/shard_map/while/body/eval_jaxpr/bgqt,btgd->bgqd/dot_general | solution.py:95
  424.0 4.0 bitcast_reduce_fusion.2
  428.0 4.6 fusion.58
  432.9 7.3 %fusion.60 = f32[2,2,1024,128]{3,2,1,0:T(8,128)} fusion(f32[2,2,1024,128]{3,2,1,0:T(8,128)} %get-tuple-element.347, f32[2,2,512,1024]{3,2,1,0:T(8,128)} %get-tuple-element.327, f32[2,2,512]{2,1,0:T(2,128)S(1)} %mul.310, f32[2,2,1024]{2,1,0:T(2,128)S(1)} %fusion.57, f32[2,2,512]{2,1,0:T(2,128)S(1)} %mul.309, ...), kind=kOutput, calls=%fused_computation.13.clone.1 | convolution fusion | flops 551026688 | bytes 13157377 | tf_op jit(solution)/shard_map/while/body/eval_jaxpr/bgqt,btgd->bgqd/dot_general | solution.py:95
  442.0 4.0 bitcast_reduce_fusion.2
  446.0 4.6 fusion.58
  450.9 7.3 %fusion.60 = f32[2,2,1024,128]{3,2,1,0:T(8,128)} fusion(f32[2,2,1024,128]{3,2,1,0:T(8,128)} %get-tuple-element.347, f32[2,2,512,1024]{3,2,1,0:T(8,128)} %get-tuple-element.327, f32[2,2,512]{2,1,0:T(2,128)S(1)} %mul.310, f32[2,2,1024]{2,1,0:T(2,128)S(1)} %fusion.57, f32[2,2,512]{2,1,0:T(2,128)S(1)} %mul.309, ...), kind=kOutput, calls=%fused_computation.13.clone.1 | convolution fusion | flops 551026688 | bytes 13157377 | tf_op jit(solution)/shard_map/while/body/eval_jaxpr/bgqt,btgd->bgqd/dot_general | solution.py:95
  460.0 4.0 bitcast_reduce_fusion.2
  464.0 4.6 fusion.58
  468.9 7.3 %fusion.60 = f32[2,2,1024,128]{3,2,1,0:T(8,128)} fusion(f32[2,2,1024,128]{3,2,1,0:T(8,128)} %get-tuple-element.347, f32[2,2,512,1024]{3,2,1,0:T(8,128)} %get-tuple-element.327, f32[2,2,512]{2,1,0:T(2,128)S(1)} %mul.310, f32[2,2,1024]{2,1,0:T(2,128)S(1)} %fusion.57, f32[2,2,512]{2,1,0:T(2,128)S(1)} %mul.309, ...), kind=kOutput, calls=%fused_computation.13.clone.1 | convolution fusion | flops 551026688 | bytes 13157377 | tf_op jit(solution)/shard_map/while/body/eval_jaxpr/bgqt,btgd->bgqd/dot_general | solution.py:95
  478.0 4.0 bitcast_reduce_fusion.2
  482.0 4.6 fusion.58
  486.9 7.3 %fusion.60 = f32[2,2,1024,128]{3,2,1,0:T(8,128)} fusion(f32[2,2,1024,128]{3,2,1,0:T(8,128)} %get-tuple-element.347, f32[2,2,512,1024]{3,2,1,0:T(8,128)} %get-tuple-element.327, f32[2,2,512]{2,1,0:T(2,128)S(1)} %mul.310, f32[2,2,1024]{2,1,0:T(2,128)S(1)} %fusion.57, f32[2,2,512]{2,1,0:T(2,128)S(1)} %mul.309, ...), kind=kOutput, calls=%fused_computation.13.clone.1 | convolution fusion | flops 551026688 | bytes 13157377 | tf_op jit(solution)/shard_map/while/body/eval_jaxpr/bgqt,btgd->bgqd/dot_general | solution.py:95
  496.1 4.0 bitcast_reduce_fusion.2
  500.1 4.6 fusion.58
  504.9 7.3 %fusion.60 = f32[2,2,1024,128]{3,2,1,0:T(8,128)} fusion(f32[2,2,1024,128]{3,2,1,0:T(8,128)} %get-tuple-element.347, f32[2,2,512,1024]{3,2,1,0:T(8,128)} %get-tuple-element.327, f32[2,2,512]{2,1,0:T(2,128)S(1)} %mul.310, f32[2,2,1024]{2,1,0:T(2,128)S(1)} %fusion.57, f32[2,2,512]{2,1,0:T(2,128)S(1)} %mul.309, ...), kind=kOutput, calls=%fused_computation.13.clone.1 | convolution fusion | flops 551026688 | bytes 13157377 | tf_op jit(solution)/shard_map/while/body/eval_jaxpr/bgqt,btgd->bgqd/dot_general | solution.py:95
  514.1 4.0 bitcast_reduce_fusion.2
  518.1 4.6 fusion.58
  523.0 7.3 %fusion.60 = f32[2,2,1024,128]{3,2,1,0:T(8,128)} fusion(f32[2,2,1024,128]{3,2,1,0:T(8,128)} %get-tuple-element.347, f32[2,2,512,1024]{3,2,1,0:T(8,128)} %get-tuple-element.327, f32[2,2,512]{2,1,0:T(2,128)S(1)} %mul.310, f32[2,2,1024]{2,1,0:T(2,128)S(1)} %fusion.57, f32[2,2,512]{2,1,0:T(2,128)S(1)} %mul.309, ...), kind=kOutput, calls=%fused_computation.13.clone.1 | convolution fusion | flops 551026688 | bytes 13157377 | tf_op jit(solution)/shard_map/while/body/eval_jaxpr/bgqt,btgd->bgqd/dot_general | solution.py:95
  532.1 4.0 bitcast_reduce_fusion.2
  536.1 4.6 fusion.58
  541.0 7.3 %fusion.60 = f32[2,2,1024,128]{3,2,1,0:T(8,128)} fusion(f32[2,2,1024,128]{3,2,1,0:T(8,128)} %get-tuple-element.347, f32[2,2,512,1024]{3,2,1,0:T(8,128)} %get-tuple-element.327, f32[2,2,512]{2,1,0:T(2,128)S(1)} %mul.310, f32[2,2,1024]{2,1,0:T(2,128)S(1)} %fusion.57, f32[2,2,512]{2,1,0:T(2,128)S(1)} %mul.309, ...), kind=kOutput, calls=%fused_computation.13.clone.1 | convolution fusion | flops 551026688 | bytes 13157377 | tf_op jit(solution)/shard_map/while/body/eval_jaxpr/bgqt,btgd->bgqd/dot_general | solution.py:95
  550.1 4.0 bitcast_reduce_fusion.2
  554.1 4.6 fusion.58
  559.0 7.3 %fusion.60 = f32[2,2,1024,128]{3,2,1,0:T(8,128)} fusion(f32[2,2,1024,128]{3,2,1,0:T(8,128)} %get-tuple-element.347, f32[2,2,512,1024]{3,2,1,0:T(8,128)} %get-tuple-element.327, f32[2,2,512]{2,1,0:T(2,128)S(1)} %mul.310, f32[2,2,1024]{2,1,0:T(2,128)S(1)} %fusion.57, f32[2,2,512]{2,1,0:T(2,128)S(1)} %mul.309, ...), kind=kOutput, calls=%fused_computation.13.clone.1 | convolution fusion | flops 551026688 | bytes 13157377 | tf_op jit(solution)/shard_map/while/body/eval_jaxpr/bgqt,btgd->bgqd/dot_general | solution.py:95
  568.1 4.0 bitcast_reduce_fusion.2
  572.1 4.6 fusion.58
  577.0 7.3 %fusion.60 = f32[2,2,1024,128]{3,2,1,0:T(8,128)} fusion(f32[2,2,1024,128]{3,2,1,0:T(8,128)} %get-tuple-element.347, f32[2,2,512,1024]{3,2,1,0:T(8,128)} %get-tuple-element.327, f32[2,2,512]{2,1,0:T(2,128)S(1)} %mul.310, f32[2,2,1024]{2,1,0:T(2,128)S(1)} %fusion.57, f32[2,2,512]{2,1,0:T(2,128)S(1)} %mul.309, ...), kind=kOutput, calls=%fused_computation.13.clone.1 | convolution fusion | flops 551026688 | bytes 13157377 | tf_op jit(solution)/shard_map/while/body/eval_jaxpr/bgqt,btgd->bgqd/dot_general | solution.py:95
  584.3 1.9 divide_convert_fusion
  586.4 5.1 fusion.18
  591.6 10.6 %all_to_all.15 = bf16[2,256,1024]{2,1,0:T(8,128)(2,1)S(1)} all-to-all(bf16[2,256,1024]{2,1,0:T(8,128)(2,1)S(1)} %bitcast.133), channel_id=1, replica_groups=mesh['sections'=4,'cache'=16,'heads'=2] {'heads'}, dimensions={0} | all-to-all | bytes 2097152 | tf_op jit(solution)/shard_map/all_to_all | solution.py:32
  603.9 13.1 %collective-permute-done = bf16[1,256,1024]{2,1,0:T(8,128)(2,1)S(1)} collective-permute-done((bf16[1,256,1024]{2,1,0:T(8,128)(2,1)S(1)}, bf16[1,256,1024]{2,1,0:T(8,128)(2,1)S(1)}, u32[]{:S(2)}, u32[]{:S(2)}) %collective-permute-start) | collective-permute-done | bytes 524320 | tf_op jit(solution)/shard_map/ppermute | solution.py:39
  (329 shorter events, 44.2 us)
Async XLA Ops:
  0.0 4.6 copy-start
  13.0 8.8 %copy-start.2 = (bf16[1,32,64,256]{3,2,1,0:T(8,128)(2,1)S(1)}, bf16[1,32,64,256]{3,2,1,0:T(8,128)(2,1)}, u32[]{:S(2)}) copy-start(bf16[1,32,64,256]{3,2,1,0:T(8,128)(2,1)} %param.21) | copy-start | bytes 3145732
  13.0 131.9 %all-to-all-start = ((bf16[16,2,8,64,256]{4,3,2,1,0:T(8,128)(2,1)}), bf16[16,2,8,64,256]{4,3,2,1,0:T(8,128)(2,1)}, u32[]{:S(2)}, u32[]{:S(2)}) async-start(bf16[16,2,8,64,256]{4,3,2,1,0:T(8,128)(2,1)} %bitcast.129), calls=%async_computation | async-start | bytes 16777216 | tf_op jit(solution)/shard_map/all_to_all | solution.py:153
  144.9 5.6 copy-start.8
  144.9 6.3 %copy-start.6 = (f32[1,32,2]{1,2,0:T(2,128)S(1)}, f32[1,32,2]{1,2,0:T(2,128)}, u32[]{:S(2)}) copy-start(f32[1,32,2]{1,2,0:T(2,128)} %param.23) | copy-start | bytes 772
  144.9 6.3 %copy-start.7 = (f32[1,32,2]{1,2,0:T(2,128)S(1)}, f32[1,32,2]{1,2,0:T(2,128)}, u32[]{:S(2)}) copy-start(f32[1,32,2]{1,2,0:T(2,128)} %param.22) | copy-start | bytes 772
  144.9 151.4 %all-to-all-start.1 = ((bf16[16,2,8,64,256]{4,3,2,1,0:T(8,128)(2,1)}), bf16[16,2,8,64,256]{4,3,2,1,0:T(8,128)(2,1)}, u32[]{:S(2)}, u32[]{:S(2)}) async-start(bf16[16,2,8,64,256]{4,3,2,1,0:T(8,128)(2,1)} %bitcast.128), calls=%async_computation.1 | async-start | bytes 16777216 | tf_op jit(solution)/shard_map/all_to_all | solution.py:154
  151.3 9.9 %copy-start.3 = (bf16[1,256,2048]{2,1,0:T(8,128)(2,1)S(1)}, bf16[1,256,2048]{2,1,0:T(8,128)(2,1)}, u32[]{:S(2)}) copy-start(bf16[1,256,2048]{2,1,0:T(8,128)(2,1)} %param.15) | copy-start | bytes 3145732
  151.3 133.4 %copy-start.5 = (f32[1,2048]{1,0:T(1,128)S(1)}, f32[1,2048]{1,0:T(1,128)}, u32[]{:S(2)}) copy-start(f32[1,2048]{1,0:T(1,128)} %param.16) | copy-start | bytes 24580
  285.1 10.3 %copy-start.9 = (f32[1,128]{1,0:T(1,128)S(1)}, f32[1,128]{1,0:T(1,128)}, u32[]{:S(2)}) copy-start(f32[1,128]{1,0:T(1,128)} %param.18) | copy-start | bytes 1540
  586.4 16.0 %copy-start.4 = (f32[1,256,2048]{2,1,0:T(8,128)S(1)}, f32[1,256,2048]{2,1,0:T(8,128)}, u32[]{:S(2)}) copy-start(f32[1,256,2048]{2,1,0:T(8,128)} %convert_element_type.72) | copy-start | bytes 6291460
  586.4 31.4 %copy-start.1 = (bf16[1,32,64,256]{3,2,1,0:T(8,128)(2,1)S(1)}, bf16[1,32,64,256]{3,2,1,0:T(8,128)(2,1)}, u32[]{:S(2)}) copy-start(bf16[1,32,64,256]{3,2,1,0:T(8,128)(2,1)} %param.20) | copy-start | bytes 3145732
  602.6 14.4 %collective-permute-start = (bf16[1,256,1024]{2,1,0:T(8,128)(2,1)S(1)}, bf16[1,256,1024]{2,1,0:T(8,128)(2,1)S(1)}, u32[]{:S(2)}, u32[]{:S(2)}) collective-permute-start(bf16[1,256,1024]{2,1,0:T(8,128)(2,1)S(1)} %fusion.24), channel_id=1, source_target_pairs={{96,0},{0,32},{32,64},{64,96},{97,1},{1,33},{33,65},{65,97},{98,2}... | collective-permute-start | bytes 1572872 | tf_op jit(solution)/shard_map/ppermute | solution.py:39
where the time goes:
time: 619 us; the launch traced here: 618 us
  matrix products  195 us (32%)
  blocking collectives  131 us (21%)
  waiting for transfers between devices  128 us (21%)
  other arithmetic  85.8 us (14%)
  local copies, waits for them, and re-layouts  61.4 us (10%)
  starting transfers between devices  15.6 us (3%)
    all_gather x1, blocking collectives, side_by_side(): whole = lax.all_gather(both, axis, axis=dim, tiled=True)  120 us
    dot_general x16, matrix products, attend(): jnp.einsum('bgqt,btgd->bgqd', scaled, value_rows, preferred_element_type=...  116 us
    all_to_all x1, waiting for transfers between devices, body(): lax.all_to_all(outgoing_keys, 'cache', split_axis=0, concat_axis=0, tiled...  115 us
    reduce_sum x16, other arithmetic, attend(): totals = totals * rescale + jnp.sum(weights, axis=-1)  73 us
    dot_general x16, matrix products, attend(): jnp.einsum('bgqd,btgd->bgqt', queries, key_rows, preferred_element_type=j...  63.6 us
    dynamic_slice x16, local copies, waits for them, and re-layouts, select_row(): return lax.dynamic_index_in_dim(stacked, source, 0, keepdims=False)  20.3 us
    ppermute x1, waiting for transfers between devices, shifted(): return lax.ppermute(block, axis, route)  13.1 us
  transfers between devices with their start and end apart: 3, of which 2 were waited for; matrix products, arithmetic and copies ran while one was open for 5% of the time, Pallas kernels for 0%

commit v1 on v0

v1 whole, which is shorter than its diff:
```python
import functools
import math

import jax
import jax.numpy as jnp
from jax import lax
from jax.experimental import pallas as pl
from jax.experimental.pallas import tpu as pltpu
from jax.sharding import PartitionSpec as P

QBLOCK = 128
QB_DEV = 2
MOST = 8
GRANULE = 16
CHUNK = 512
QTILE = 256

tiny_eps = 1e-06
masked_score = -1e30
lowest = -1e38


def lookup(entries, table):
    places = jnp.arange(table.shape[0], dtype=jnp.int32)
    return jnp.sum(jnp.where(entries[..., None] == places, table, 0), axis=-1)


def ranked(chosen):
    listed = chosen.shape[-1]
    order = jnp.arange(listed, dtype=jnp.int32)
    before = order[:, None] < order[None, :]
    ranks = jnp.sum(jnp.where(before & chosen[..., :, None], 1, 0), axis=-2)
    wanted = jnp.arange(MOST, dtype=jnp.int32)
    return (ranks[..., None, :] == wanted[:, None]) & chosen[..., None, :]


def pick(picks, values):
    return jnp.sum(jnp.where(picks, values[..., None, :], 0), axis=-1)


def pack_kernel(cnt_ref, rows_ref, page_ref, k_ref, v_ref, out_ref, buf, sems, *, page_len):
    homes, height, _ = out_ref.shape
    head_size = k_ref.shape[1]

    def copy_of(home, slot):
        return pltpu.make_async_copy(buf.at[slot, pl.ds(0, height), :], out_ref.at[home], sems.at[slot])

    def one_home(home, carry):
        slot = lax.rem(home, 2)

        @pl.when(home >= 2)
        def _():
            copy_of(home - 2, slot).wait()

        row = jnp.int32(0)
        for b in range(QB_DEV):
            block = home * QB_DEV + b

            def one_page(j, row, block=block):
                at = block * MOST + j
                here = pl.multiple_of(page_ref[at] * page_len, page_len)
                there = pl.multiple_of(row, GRANULE)
                buf[slot, pl.ds(there, page_len), 0:head_size] = k_ref[pl.ds(here, page_len), :]
                buf[slot, pl.ds(there, page_len), head_size : 2 * head_size] = v_ref[pl.ds(here, page_len), :]
                return row + rows_ref[at]

            row = lax.fori_loop(0, cnt_ref[block], one_page, row)
        copy_of(home, slot).start()
        return carry

    lax.fori_loop(0, homes, one_home, 0)
    copy_of(homes - 2, 0).wait()
    copy_of(homes - 1, 1).wait()


def pack(cnt, rows, pages, key_rows, value_rows, g, homes, height, page_len, head_size):
    tokens = key_rows.shape[0]
    return pl.pallas_call(
        functools.partial(pack_kernel, page_len=page_len),
        grid_spec=pltpu.PrefetchScalarGridSpec(
            num_scalar_prefetch=3,
            grid=(1,),
            in_specs=[
                pl.BlockSpec((tokens, head_size), lambda i, *_: (0, g)),
                pl.BlockSpec((tokens, head_size), lambda i, *_: (0, g)),
            ],
            out_specs=pl.BlockSpec(memory_space=pl.ANY),
            scratch_shapes=[
                pltpu.VMEM((2, height + page_len, 2 * head_size), jnp.bfloat16),
                pltpu.SemaphoreType.DMA((2,)),
            ],
        ),
        out_shape=jax.ShapeDtypeStruct((homes, height, 2 * head_size), jnp.bfloat16),
        compiler_params=pltpu.CompilerParams(vmem_limit_bytes=24 << 20),
        cost_estimate=pl.CostEstimate(
            flops=0, transcendentals=0, bytes_accessed=homes * height * 4 * head_size + tokens * 4 * head_size
        ),
    )(cnt, rows, pages, key_rows, value_rows)


def attend_kernel(
    cnt_ref, first_ref, height_ref, rows_ref, live_ref, kscale_ref, vscale_ref,
    qt_ref, recv_ref, out_ref,
    kv, kcol, vcol, bias, acc, top, total, sems, *, page_len,
):
    sources = recv_ref.shape[0]
    head_size, width = qt_ref.shape

    def copy_of(s, at):
        n = pl.multiple_of(height_ref[s], GRANULE)
        start = pl.multiple_of(first_ref[s], GRANULE)
        at = pl.multiple_of(at, GRANULE)
        return pltpu.make_async_copy(
            recv_ref.at[s, pl.ds(start, n), :], kv.at[pl.ds(at, n), :], sems.at[s]
        )

    def start_one(s, at):
        @pl.when(height_ref[s] > 0)
        def _():
            copy_of(s, at).start()

        return at + height_ref[s]

    def wait_one(s, at):
        @pl.when(height_ref[s] > 0)
        def _():
            copy_of(s, at).wait()

        return at + height_ref[s]

    used = lax.fori_loop(0, sources, start_one, jnp.int32(0))
    token = lax.broadcasted_iota(jnp.int32, (page_len, 128), 0)

    def columns_of(s, at):
        def one_page(j, at):
            e = s * MOST + j
            here = pl.ds(pl.multiple_of(at, GRANULE), page_len)
            kcol[here, :] = jnp.full((page_len, 128), kscale_ref[e], jnp.float32)
            vcol[here, :] = jnp.full((page_len, 128), vscale_ref[e], jnp.float32)
            bias[here, :] = jnp.where(token < live_ref[e], 0.0, masked_score)
            return at + rows_ref[e]

        return lax.fori_loop(0, cnt_ref[s], one_page, at)

    lax.fori_loop(0, sources, columns_of, jnp.int32(0))
    rest = pl.ds(pl.multiple_of(used, GRANULE), CHUNK)
    kcol[rest, :] = jnp.zeros((CHUNK, 128), jnp.float32)
    vcol[rest, :] = jnp.zeros((CHUNK, 128), jnp.float32)
    bias[rest, :] = jnp.full((CHUNK, 128), masked_score, jnp.float32)
    kv[rest, :] = jnp.zeros((CHUNK, 2 * head_size), jnp.bfloat16)
    acc[...] = jnp.zeros_like(acc)
    total[...] = jnp.zeros_like(total)
    top[...] = jnp.full_like(top, lowest)
    lax.fori_loop(0, sources, wait_one, jnp.int32(0))

    def chunk(c, carry):
        here = pl.ds(pl.multiple_of(c * CHUNK, CHUNK), CHUNK)
        keys = kv[here, 0:head_size]
        values = kv[here, head_size : 2 * head_size].T
        for i in range(width // QTILE):
            cols = pl.ds(i * QTILE, QTILE)
            score = jnp.dot(keys, qt_ref[:, cols], preferred_element_type=jnp.float32)
            kc, bc, vc = kcol[here, :], bias[here, :], vcol[here, :]
            wide = lambda x: jnp.concatenate([x] * (QTILE // 128), axis=1)
            score = score * wide(kc) + wide(bc)
            old = top[0:1, cols]
            new = jnp.maximum(old, jnp.max(score, axis=0, keepdims=True))
            weight = jnp.exp2(score - new)
            fade = jnp.exp2(old - new)
            total[0:1, cols] = total[0:1, cols] * fade + jnp.sum(weight, axis=0, keepdims=True)
            scaled = (weight * wide(vc)).astype(jnp.bfloat16)
            acc[:, cols] = acc[:, cols] * fade + jnp.dot(values, scaled, preferred_element_type=jnp.float32)
            top[0:1, cols] = new
        return carry

    lax.fori_loop(0, (used + CHUNK - 1) // CHUNK, chunk, 0)
    for h in range(width // QBLOCK):
        cols = slice(h * QBLOCK, (h + 1) * QBLOCK)
        out_ref[:, h * head_size : (h + 1) * head_size] = (acc[:, cols] / total[0:1, cols]).T.astype(jnp.bfloat16)


def attend(plan, qt, received, page_len, most_rows):
    head_size, width = qt.shape
    sources = received.shape[0]
    rows_held = most_rows + CHUNK + page_len
    out_width = width // QBLOCK * head_size
    return pl.pallas_call(
        functools.partial(attend_kernel, page_len=page_len),
        grid_spec=pltpu.PrefetchScalarGridSpec(
            num_scalar_prefetch=7,
            grid=(1,),
            in_specs=[
                pl.BlockSpec((head_size, width), lambda i, *_: (0, 0)),
                pl.BlockSpec(memory_space=pl.ANY),
            ],
            out_specs=pl.BlockSpec((QBLOCK, out_width), lambda i, *_: (0, 0)),
            scratch_shapes=[
                pltpu.VMEM((rows_held, 2 * head_size), jnp.bfloat16),
                pltpu.VMEM((rows_held, 128), jnp.float32),
                pltpu.VMEM((rows_held, 128), jnp.float32),
                pltpu.VMEM((rows_held, 128), jnp.float32),
                pltpu.VMEM((head_size, width), jnp.float32),
                pltpu.VMEM((8, width), jnp.float32),
                pltpu.VMEM((8, width), jnp.float32),
                pltpu.SemaphoreType.DMA((sources,)),
            ],
        ),
        out_shape=jax.ShapeDtypeStruct((QBLOCK, out_width), jnp.bfloat16),
        compiler_params=pltpu.CompilerParams(vmem_limit_bytes=40 << 20),
        cost_estimate=pl.CostEstimate(
            flops=4 * width * most_rows * head_size,
            transcendentals=width * most_rows,
            bytes_accessed=most_rows * 4 * head_size + width * head_size * 4,
        ),
    )(*plan, qt, received)


def body(
    hidden,
    norm_gain,
    w_query,
    query_gain,
    w_output,
    key_cache,
    value_cache,
    key_scale,
    value_scale,
    page_table,
    page_tokens,
    page_list,
    list_len,
):
    row_count, model_width = hidden.shape[1:]
    head_size = query_gain.shape[1]
    kv_local = key_scale.shape[2]
    heads_local = w_query.shape[2] // head_size
    group_size = heads_local // kv_local
    pages_dev, page_len = key_cache.shape[1:3]
    listed = page_list.shape[2]
    shard_count = lax.axis_size("cache")
    own_shard = lax.axis_index("cache")
    height = QB_DEV * MOST * page_len

    entry = lookup(page_list[0], page_table * 128 + page_tokens)
    slots, counts = entry // 128, entry % 128
    used = jnp.arange(listed, dtype=jnp.int32) < list_len[0][:, None]
    rows = (counts + GRANULE - 1) // GRANULE * GRANULE
    mine = (slots // pages_dev == own_shard) & used
    picks = ranked(mine)
    send_cnt = jnp.sum(mine.astype(jnp.int32), axis=-1)
    send_rows = pick(picks, rows).reshape(-1)
    send_page = pick(picks, slots % pages_dev).reshape(-1)

    key_rows = key_cache[0].reshape(pages_dev * page_len, -1)
    value_rows = value_cache[0].reshape(pages_dev * page_len, -1)
    received = []
    for g in range(kv_local):
        out = pack(
            send_cnt, send_rows, send_page, key_rows, value_rows, g, shard_count, height, page_len, head_size
        )
        if g > 0:
            out, received[-1] = lax.optimization_barrier((out, received[-1]))
        received.append(lax.all_to_all(out, "cache", split_axis=0, concat_axis=0, tiled=True))

    scales = lax.all_gather(jnp.concatenate([key_scale[0], value_scale[0]], axis=1), "cache", axis=0, tiled=True)
    first_block = own_shard * QB_DEV

    def own(x):
        return lax.dynamic_slice_in_dim(x, first_block, QB_DEV, 0)

    own_slots, own_counts, own_rows, own_used = own(slots), own(counts), own(rows), own(used)
    sources = jnp.arange(shard_count, dtype=jnp.int32)
    theirs = (own_slots[:, None, :] // pages_dev == sources[:, None]) & own_used[:, None, :]
    own_picks = ranked(theirs)
    got_cnt = jnp.sum(theirs.astype(jnp.int32), axis=-1)
    got_height = jnp.sum(jnp.where(theirs, own_rows[:, None, :], 0), axis=-1)
    got_first = jnp.stack([jnp.zeros_like(got_height[0]), got_height[0]])
    got_rows = pick(own_picks, own_rows[:, None, :]).reshape(QB_DEV, -1)
    got_live = pick(own_picks, own_counts[:, None, :]).reshape(QB_DEV, -1)
    places = jnp.arange(scales.shape[0], dtype=jnp.int32)
    at_place = own_slots[..., None] == places
    got_scales = [
        pick(own_picks, jnp.sum(jnp.where(at_place, scales[:, k], 0.0), axis=-1)[:, None, :]).reshape(QB_DEV, -1)
        for k in range(2 * kv_local)
    ]

    inputs = hidden[0].astype(jnp.float32)
    inverse = lax.rsqrt(jnp.mean(inputs * inputs, axis=-1, keepdims=True) + tiny_eps)
    normed = (inputs * inverse * norm_gain[0]).astype(jnp.bfloat16)
    projected = jnp.dot(normed, w_query[0], preferred_element_type=jnp.float32)
    projected = projected.reshape(QB_DEV, QBLOCK, kv_local, group_size, head_size)
    head_inverse = lax.rsqrt(jnp.mean(projected * projected, axis=-1, keepdims=True) + tiny_eps)
    queries = (projected * head_inverse * query_gain[0] / math.sqrt(head_size)).astype(jnp.bfloat16)
    queries = jnp.transpose(queries, (0, 2, 4, 3, 1)).reshape(QB_DEV, kv_local, head_size, group_size * QBLOCK)

    span = group_size * head_size
    heads_index = lax.axis_index("heads")
    half_width = model_width // lax.axis_size("heads")
    devices = lax.axis_size("sections")
    partial = [None] * QB_DEV
    for g in range(kv_local):
        for b in range(QB_DEV):
            plan = (
                got_cnt[b],
                got_first[b],
                got_height[b],
                got_rows[b],
                got_live[b],
                got_scales[g][b] * math.log2(math.e),
                got_scales[kv_local + g][b],
            )
            attended = attend(plan, queries[b, g], received[g], page_len, listed * page_len)
            term = jnp.dot(attended, w_output[0, g * span : (g + 1) * span], preferred_element_type=jnp.float32)
            partial[b] = term if g == 0 else partial[b] + term
    moved = []
    for b in range(QB_DEV):
        whole = partial[b]
        away = lax.dynamic_slice_in_dim(whole, (1 - heads_index) * half_width, half_width, 1)
        came = lax.ppermute(away.astype(jnp.bfloat16), "heads", [(0, 1), (1, 0)])
        kept = lax.dynamic_slice_in_dim(whole, heads_index * half_width, half_width, 1)
        residual = lax.dynamic_slice(
            inputs, (b * QBLOCK, heads_index * half_width), (QBLOCK, half_width)
        )
        result = (kept + came.astype(jnp.float32) + residual).astype(jnp.bfloat16)
        moved.append(lax.ppermute(result, "sections", [((i - 1) % devices, i) for i in range(devices)]))
    return jnp.concatenate(moved, axis=0)[None]


def solution(mesh):
    return jax.shard_map(
        body,
        mesh=mesh,
        in_specs=(
            P("sections", "cache", None),
            P("sections", None),
            P("sections", None, "heads"),
            P("sections", None),
            P("sections", "heads", None),
            P("sections", "cache", None, "heads"),
            P("sections", "cache", None, "heads"),
            P("sections", "cache", "heads"),
            P("sections", "cache", "heads"),
            P(),
            P(),
            P("sections", None, None),
            P("sections", None),
        ),
        out_specs=P("sections", "cache", "heads"),
        check_vma=False,
    )
```

time: 619 us -> 385 us (0.62)
  matrix products: 195 us -> 12.5 us
  other arithmetic: 85.8 us -> 11.2 us
  Pallas kernels: 0 us -> 46.7 us
  local copies, waits for them, and re-layouts: 61.4 us -> 24.5 us
  starting transfers between devices: 15.6 us -> 26.6 us
    dot_general x36 -> x5, matrix products: 195 us -> 12.5 us  [the longest x4 7.43 us: body(): jnp.dot(attended, w_output[0, g * span:(g + 1) * span], preferred_element...]
    reduce_sum x20 -> x9, other arithmetic: 77.9 us -> 6.28 us  [the longest x3 2.53 us: pick(): return jnp.sum(jnp.where(picks, values[..., None, :], 0), axis=-1)]
    pallas_call x0 -> x6, Pallas kernels: none -> 46.7 us  [the longest x4 40 us: attend(): pl.pallas_call(functools.partial(attend_kernel, page_len=page_len), grid_...]
    dynamic_slice x16 -> x2, local copies, waits for them, and re-layouts: 20.3 us -> 0.02 us  [own(): return lax.dynamic_slice_in_dim(x, first_block, QB_DEV, 0)]
    gather x2 -> x0, local copies, waits for them, and re-layouts: 16.8 us -> none  [the longest x1 8.39 us: body(): outgoing_values = value_cache[0][local_all].reshape(page_shape)]
    dot_general x1, local copies, waits for them, and re-layouts: 0.1 us -> 12.4 us  [body(): projected = jnp.dot(normed, w_query[0], preferred_element_type=jnp.float32)]
    ppermute x1 -> x4, starting transfers between devices: 1.29 us -> 12.8 us  [the longest x2 7.76 us: body(): came = lax.ppermute(away.astype(jnp.bfloat16), 'heads', [(0, 1), (1, 0)])]
    all_to_all x1 -> x0, blocking collectives: 10.6 us -> none  [sum_at_owner(): lax.all_to_all(parts, axis, split_axis=0, concat_axis=0, tiled=True)]
  transfers between devices with their start and end apart: 3 -> 6, of which waited for: 2 -> 4; matrix products, arithmetic and copies ran while one was open for 5% -> 7% of each run, Pallas kernels for 0% -> 9%
where the time goes in v1:
time: 385 us; the launch traced here: 380 us
  blocking collectives  130 us (34%)
  waiting for transfers between devices  129 us (34%)
  Pallas kernels  46.7 us (12%)
  starting transfers between devices  26.6 us (7%)
  local copies, waits for them, and re-layouts  24.5 us (6%)
  matrix products  12.5 us (3%)
  other arithmetic  11.2 us (3%)
    all_gather x1, blocking collectives, body(): lax.all_gather(jnp.concatenate([key_scale[0], value_scale[0]], axis=1), '...  130 us
    all_to_all x2, waiting for transfers between devices, body(): lax.all_to_all(out, 'cache', split_axis=0, concat_axis=0, tiled=True)  116 us
    pallas_call x4, Pallas kernels, attend(): pl.pallas_call(functools.partial(attend_kernel, page_len=page_len), grid_...  40 us
    all_to_all x2, starting transfers between devices, body(): lax.all_to_all(out, 'cache', split_axis=0, concat_axis=0, tiled=True)  13.8 us
    dot_general x1, local copies, waits for them, and re-layouts, body(): projected = jnp.dot(normed, w_query[0], preferred_element_type=jnp.float32)  12.4 us
    ppermute x2, waiting for transfers between devices, body(): lax.ppermute(result, 'sections', [((i - 1) % devices, i) for i in range(d...  10.9 us
    unnamed x37, local copies, waits for them, and re-layouts  9.84 us
    ppermute x2, starting transfers between devices, body(): came = lax.ppermute(away.astype(jnp.bfloat16), 'heads', [(0, 1), (1, 0)])  7.76 us
  transfers between devices with their start and end apart: 6, of which 4 were waited for; matrix products, arithmetic and copies ran while one was open for 7% of the time, Pallas kernels for 9%

profile of v1, /device:TPU:1, one launch (start us, length us, event | category | flops | bytes accessed | tf_op | source)
XLA Modules:
  0.0 380.2 jit_solution(6047647908340774820)
XLA Ops:
  0.0 0.7 multiply_add_fusion
  0.7 1.8 select_reduce_fusion
  2.6 0.8 convert_reduce_fusion
  3.4 0.4 select_reduce_fusion.1
  3.8 1.2 select_reduce_fusion.9
  4.9 0.1 reshape.313.rows_ref
  5.0 0.1 reshape.314.page_ref
  5.1 1.2 copy-done.2
  6.4 1.2 copy-done.4
  7.6 3.4 shard_map.128
  11.0 3.2 copy-done.1
  14.2 8.4 %all-to-all-start = ((bf16[16,1024,256]{2,1,0:T(8,128)(2,1)}), bf16[16,1024,256]{2,1,0:T(8,128)(2,1)}, u32[]{:S(2)}, u32[]{:S(2)}) async-start(bf16[16,1024,256]{2,1,0:T(8,128)(2,1)} %copy-done.1), calls=%async_computation | async-start | bytes 16777216 | tf_op jit(solution)/shard_map/all_to_all | solution.py:263
  22.6 3.4 shard_map.127
  26.0 3.2 copy-done
  29.2 116.5 %all-to-all-done.recv_ref = bf16[16,1024,256]{2,1,0:T(8,128)(2,1)} async-done(((bf16[16,1024,256]{2,1,0:T(8,128)(2,1)}), bf16[16,1024,256]{2,1,0:T(8,128)(2,1)}, u32[]{:S(2)}, u32[]{:S(2)}) %all-to-all-start) | async-done | bytes 8388640 | tf_op jit(solution)/shard_map/all_to_all | solution.py:263
  145.7 5.4 %all-to-all-start.1 = ((bf16[16,1024,256]{2,1,0:T(8,128)(2,1)}), bf16[16,1024,256]{2,1,0:T(8,128)(2,1)}, u32[]{:S(2)}, u32[]{:S(2)}) async-start(bf16[16,1024,256]{2,1,0:T(8,128)(2,1)} %copy-done), calls=%async_computation.1 | async-start | bytes 16777216 | tf_op jit(solution)/shard_map/all_to_all | solution.py:263
  151.3 0.4 select_reduce_fusion.2
  151.7 1.2 select_reduce_fusion.13
  152.9 0.1 squeeze.92.rows_ref
  153.0 0.1 squeeze.93.live_ref
  153.1 129.5 %all-gather = f32[16,32,4]{1,2,0:T(4,128)S(1)} all-gather(f32[1,32,4]{1,2,0:T(4,128)S(1)} %maximum_bitcast_fusion.1), channel_id=1, replica_groups=mesh['sections'=4,'cache'=16,'heads'=2] {'cache'}, dimensions={0}, use_global_device_ids=true | all-gather | bytes 8704 | tf_op jit(solution)/shard_map/all_gather | solution.py:265
  282.6 0.1 reshape.316
  282.7 0.2 select_reduce_fusion.5
  283.0 0.2 select_reduce_fusion.11
  283.2 0.1 mul.122.kscale_ref
  283.3 0.1 squeeze.104.vscale_ref
  283.4 12.4 %copy.26 = bf16[2048,2048]{1,0:T(8,128)(2,1)} copy(bf16[2048,2048]{0,1:T(8,128)(2,1)} %bitcast.88) | data formatting | bytes 16777216 | tf_op jit(solution)/shard_map/dot_general | solution.py:290
  295.8 0.3 multiply_reduce_fusion.1
  296.2 0.3 multiply_convert_fusion
  296.5 5.1 %multiply_reduce_fusion = (f32[2,128,2,8]{1,3,2,0:T(8,128)S(1)}, f32[2,128,2,8,128]{4,1,3,2,0:T(8,128)S(1)}) fusion(bf16[2,128,2048,1,1]{2,1,4,3,0:T(8,128)(2,1)S(1)} %bitcast.93, bf16[2,8,128,2048,1]{3,2,1,0,4:T(8,128)(2,1)} %bitcast.91), kind=kOutput, calls=%fused_computation.20 | convolution fusion | flops 2148528128 | bytes 11550720 | tf_op jit(solution)/shard_map/dot_general | solution.py:290
  301.6 0.7 fusion.20
  302.4 0.1 copy.29
  302.6 0.1 mul.108.kscale_ref
  302.7 0.1 squeeze.98.vscale_ref
  302.7 0.1 copy.28
  302.9 0.1 squeeze.109.rows_ref
  303.0 0.1 squeeze.110.live_ref
  303.1 0.1 mul.128.kscale_ref
  303.2 0.1 squeeze.113.vscale_ref
  303.3 0.1 copy.31
  303.4 0.1 mul.126.kscale_ref
  303.5 0.1 squeeze.111.vscale_ref
  303.6 0.2 copy.30
  303.8 0.1 select_reduce_fusion.15
  303.9 10.8 %shard_map.129 = bf16[128,1024]{1,0:T(8,128)(2,1)S(1)} custom-call(s32[16]{0:T(128)S(1)} %get-tuple-element.55.cnt_ref, s32[16]{0:T(128)S(1)} %broadcast_6_first_ref.2.first_ref, s32[16]{0:T(128)S(1)} %get-tuple-element.58.height_ref.first_ref, s32[128]{0:T(128)S(1)} %squeeze.92.rows_ref, s32[128]{0:T(128)S(1)} %squeeze.93.live_ref, ...), custom_call_target="tpu_custom_call" | custom-call | flops 2147483648 | bytes 2621440 | tf_op jit(solution)/shard_map/pallas_call | solution.py:187
  314.8 9.0 %shard_map.131 = bf16[128,1024]{1,0:T(8,128)(2,1)S(1)} custom-call(s32[16]{0:T(128)S(1)} %get-tuple-element.56.cnt_ref, s32[16]{0:T(128)S(1)} %get-tuple-element.58.height_ref.first_ref, s32[16]{0:T(128)S(1)} %get-tuple-element.57.height_ref, s32[128]{0:T(128)S(1)} %squeeze.109.rows_ref, s32[128]{0:T(128)S(1)} %squeeze.110.live_ref, ...), custom_call_target="tpu_custom_call" | custom-call | flops 2147483648 | bytes 2621440 | tf_op jit(solution)/shard_map/pallas_call | solution.py:187
  323.8 10.9 %shard_map.130 = bf16[128,1024]{1,0:T(8,128)(2,1)S(1)} custom-call(s32[16]{0:T(128)S(1)} %get-tuple-element.55.cnt_ref, s32[16]{0:T(128)S(1)} %broadcast_6_first_ref.2.first_ref, s32[16]{0:T(128)S(1)} %get-tuple-element.58.height_ref.first_ref, s32[128]{0:T(128)S(1)} %squeeze.92.rows_ref, s32[128]{0:T(128)S(1)} %squeeze.93.live_ref, ...), custom_call_target="tpu_custom_call" | custom-call | flops 2147483648 | bytes 2621440 | tf_op jit(solution)/shard_map/pallas_call | solution.py:187
  334.7 2.9 fusion.2
  337.6 3.1 fusion.12
  340.8 6.8 %collective-permute-start = (bf16[128,1024]{1,0:T(8,128)(2,1)S(1)}, bf16[128,1024]{1,0:T(8,128)(2,1)}, u32[]{:S(2)}, u32[]{:S(2)}) collective-permute-start(bf16[128,1024]{1,0:T(8,128)(2,1)S(1)} %dynamic-slice_convert_fusion.1), channel_id=1, source_target_pairs={{0,1},{1,0},{2,3},{3,2},{4,5},{5,4},{6,7},{7,6},{8,9},{9,8},{10,11... | collective-permute-start | bytes 786440 | tf_op jit(solution)/shard_map/ppermute | solution.py:319
  347.6 9.2 %shard_map.132 = bf16[128,1024]{1,0:T(8,128)(2,1)S(1)} custom-call(s32[16]{0:T(128)S(1)} %get-tuple-element.56.cnt_ref, s32[16]{0:T(128)S(1)} %get-tuple-element.58.height_ref.first_ref, s32[16]{0:T(128)S(1)} %get-tuple-element.57.height_ref, s32[128]{0:T(128)S(1)} %squeeze.109.rows_ref, s32[128]{0:T(128)S(1)} %squeeze.110.live_ref, ...), custom_call_target="tpu_custom_call" | custom-call | flops 2147483648 | bytes 2621440 | tf_op jit(solution)/shard_map/pallas_call | solution.py:187
  356.9 0.7 fusion
  357.6 0.7 fusion.15
  358.4 0.8 dynamic-slice_convert_fusion
  359.2 0.2 copy-done.8
  359.4 0.9 collective-permute-start.2
  360.3 0.2 convert_element_type.55
  360.6 1.2 collective-permute-done.2
  361.9 1.6 fusion.22
  363.5 5.0 %collective-permute-start.3 = (bf16[128,1024]{1,0:T(8,128)(2,1)S(1)}, bf16[128,1024]{1,0:T(8,128)(2,1)S(1)}, u32[]{:S(2)}, u32[]{:S(2)}) collective-permute-start(bf16[128,1024]{1,0:T(8,128)(2,1)S(1)} %get-tuple-element.30), channel_id=1, source_target_pairs={{96,0},{0,32},{32,64},{64,96},{97,1},{1,33},{33,65},{65,97},{98,2}... | collective-permute-start | bytes 786440 | tf_op jit(solution)/shard_map/ppermute | solution.py:325
  368.5 0.1 collective-permute-start.1
  368.5 5.2 %collective-permute-done.3 = bf16[128,1024]{1,0:T(8,128)(2,1)S(1)} collective-permute-done((bf16[128,1024]{1,0:T(8,128)(2,1)S(1)}, bf16[128,1024]{1,0:T(8,128)(2,1)S(1)}, u32[]{:S(2)}, u32[]{:S(2)}) %collective-permute-start.3) | collective-permute-done | bytes 262176 | tf_op jit(solution)/shard_map/ppermute | solution.py:325
  373.8 5.6 %collective-permute-done.1 = bf16[128,1024]{1,0:T(8,128)(2,1)S(1)} collective-permute-done((bf16[128,1024]{1,0:T(8,128)(2,1)S(1)}, bf16[128,1024]{1,0:T(8,128)(2,1)S(1)}, u32[]{:S(2)}, u32[]{:S(2)}) %collective-permute-start.1) | collective-permute-done | bytes 262176 | tf_op jit(solution)/shard_map/ppermute | solution.py:325
  379.4 0.8 maximum_bitcast_fusion
  (51 shorter events, 0.4 us)
Async XLA Ops:
  5.1 1.2 copy-start.2
  6.3 1.2 copy-start.4
  11.0 3.2 copy-start.1
  14.2 8.4 %copy-start.3 = (bf16[1,32,64,256]{3,2,1,0:T(8,128)(2,1)S(1)}, bf16[1,32,64,256]{3,2,1,0:T(8,128)(2,1)}, u32[]{:S(2)}) copy-start(bf16[1,32,64,256]{3,2,1,0:T(8,128)(2,1)} %param.18) | copy-start | bytes 3145732
  14.2 8.4 %copy-start.5 = (bf16[1,32,64,256]{3,2,1,0:T(8,128)(2,1)S(1)}, bf16[1,32,64,256]{3,2,1,0:T(8,128)(2,1)}, u32[]{:S(2)}) copy-start(bf16[1,32,64,256]{3,2,1,0:T(8,128)(2,1)} %param.19) | copy-start | bytes 3145732
  14.2 131.5 %all-to-all-start = ((bf16[16,1024,256]{2,1,0:T(8,128)(2,1)}), bf16[16,1024,256]{2,1,0:T(8,128)(2,1)}, u32[]{:S(2)}, u32[]{:S(2)}) async-start(bf16[16,1024,256]{2,1,0:T(8,128)(2,1)} %copy-done.1), calls=%async_computation | async-start | bytes 16777216 | tf_op jit(solution)/shard_map/all_to_all | solution.py:263
  26.0 3.2 copy-start
  29.2 122.0 %copy-start.10 = (s32[1,32]{1,0:T(1,128)S(1)}, s32[1,32]{1,0:T(1,128)}, u32[]{:S(2)}) copy-start(s32[1,32]{1,0:T(1,128)} %param.25) | copy-start | bytes 388
  29.2 123.9 %copy-start.11 = (f32[1,32,2]{1,2,0:T(2,128)S(1)}, f32[1,32,2]{1,2,0:T(2,128)}, u32[]{:S(2)}) copy-start(f32[1,32,2]{1,2,0:T(2,128)} %param.21) | copy-start | bytes 772
  29.2 123.9 %copy-start.12 = (f32[1,32,2]{1,2,0:T(2,128)S(1)}, f32[1,32,2]{1,2,0:T(2,128)}, u32[]{:S(2)}) copy-start(f32[1,32,2]{1,2,0:T(2,128)} %param.20) | copy-start | bytes 772
  145.7 178.1 %all-to-all-start.1 = ((bf16[16,1024,256]{2,1,0:T(8,128)(2,1)}), bf16[16,1024,256]{2,1,0:T(8,128)(2,1)}, u32[]{:S(2)}, u32[]{:S(2)}) async-start(bf16[16,1024,256]{2,1,0:T(8,128)(2,1)} %copy-done), calls=%async_computation.1 | async-start | bytes 16777216 | tf_op jit(solution)/shard_map/all_to_all | solution.py:263
  283.4 12.5 %copy-start.6 = (bf16[1,256,2048]{2,1,0:T(8,128)(2,1)S(1)}, bf16[1,256,2048]{2,1,0:T(8,128)(2,1)}, u32[]{:S(2)}) copy-start(bf16[1,256,2048]{2,1,0:T(8,128)(2,1)} %param.13) | copy-start | bytes 3145732
  283.4 12.7 %copy-start.9 = (f32[1,2048]{1,0:T(1,128)S(1)}, f32[1,2048]{1,0:T(1,128)}, u32[]{:S(2)}) copy-start(f32[1,2048]{1,0:T(1,128)} %param.14) | copy-start | bytes 24580
  296.5 5.1 %copy-start.13 = (f32[1,128]{1,0:T(1,128)S(1)}, f32[1,128]{1,0:T(1,128)}, u32[]{:S(2)}) copy-start(f32[1,128]{1,0:T(1,128)} %param.16) | copy-start | bytes 1540
  337.6 19.2 %slice-start = ((s8[8388608]{0:T(1024)(128)(4,1)}), s8[4194304]{0:T(1024)(128)(4,1)S(1)}, s32[]{:S(2)}) async-start(s8[8388608]{0:T(1024)(128)(4,1)} %bitcast.89), calls=%async_computation.2 | async-start | bytes 8388608
  340.7 6.9 %copy-start.7 = (f32[128,2048]{1,0:T(8,128)}, f32[128,2048]{1,0:T(8,128)S(1)}, u32[]{:S(2)}) copy-start(f32[128,2048]{1,0:T(8,128)S(1)} %fusion.12) | copy-start | bytes 3145732
  340.8 19.8 %collective-permute-start = (bf16[128,1024]{1,0:T(8,128)(2,1)S(1)}, bf16[128,1024]{1,0:T(8,128)(2,1)}, u32[]{:S(2)}, u32[]{:S(2)}) collective-permute-start(bf16[128,1024]{1,0:T(8,128)(2,1)S(1)} %dynamic-slice_convert_fusion.1), channel_id=1, source_target_pairs={{0,1},{1,0},{2,3},{3,2},{4,5},{5,4},{6,7},{7,6},{8,9},{9,8},{10,11... | collective-permute-start | bytes 786440 | tf_op jit(solution)/shard_map/ppermute | solution.py:319
  347.6 9.3 %slice-start.1 = ((s8[8388608]{0:T(1024)(128)(4,1)}), s8[4194304]{0:T(1024)(128)(4,1)S(1)}, s32[]{:S(2)}) async-start(s8[8388608]{0:T(1024)(128)(4,1)} %bitcast.89), calls=%async_computation.3 | async-start | bytes 8388608
  358.3 1.1 copy-start.8
  359.4 2.4 collective-permute-start.2
  363.5 10.3 %collective-permute-start.3 = (bf16[128,1024]{1,0:T(8,128)(2,1)S(1)}, bf16[128,1024]{1,0:T(8,128)(2,1)S(1)}, u32[]{:S(2)}, u32[]{:S(2)}) collective-permute-start(bf16[128,1024]{1,0:T(8,128)(2,1)S(1)} %get-tuple-element.30), channel_id=1, source_target_pairs={{96,0},{0,32},{32,64},{64,96},{97,1},{1,33},{33,65},{65,97},{98,2}... | collective-permute-start | bytes 786440 | tf_op jit(solution)/shard_map/ppermute | solution.py:325
  368.5 10.9 %collective-permute-start.1 = (bf16[128,1024]{1,0:T(8,128)(2,1)S(1)}, bf16[128,1024]{1,0:T(8,128)(2,1)S(1)}, u32[]{:S(2)}, u32[]{:S(2)}) collective-permute-start(bf16[128,1024]{1,0:T(8,128)(2,1)S(1)} %get-tuple-element.29), channel_id=1, source_target_pairs={{96,0},{0,32},{32,64},{64,96},{97,1},{1,33},{33,65},{65,97},{98,2}... | collective-permute-start | bytes 786440 | tf_op jit(solution)/shard_map/ppermute | solution.py:325
